TPU v7x, 128 devices: a whole 4x4x4 slice. The times are simulated.
128 devices in a mesh: dp: 16 (over y_lo, x, core), tensor: 8 (over y_hi, z).
Axes of the slice: x: 4, y: 4 (y_hi: 2, y_lo: 2; y = y_hi * 2 + y_lo), z: 4, core: 2. Of those that a mesh axis runs over, the one named last changes fastest.
Arguments:
- picture_encoder_result: bfloat16 [5632, 1024], P('dp'), may hold values from -0.59765625 to 0.59765625
- sentence_encoder_result: bfloat16 [22528, 1024], P(('dp', 'tensor')), may hold values from -0.59765625 to 0.59765625
- picture_projector_matrix: bfloat16 [1024, 1024], P(None, 'tensor'), may hold values from -0.1875 to 0.1875
- sentence_projector_matrix: bfloat16 [1024, 1024], P(None, 'tensor'), may hold values from -0.1875 to 0.1875
- sentences_for_picture: int32 [5632], replicated, may hold values from 1 to 8, 22528 in all
- sharpness_factor: float32 [1], replicated, may hold values from 30 to 60
- score_offset_term: float32 [1], replicated, may hold values from -8 to -4
Outputs:
- grad_img: bfloat16 [5632, 1024], P('dp', 'tensor')
- grad_cap: bfloat16 [22528, 1024], P(('dp', 'tensor'))
Inputs may be any that keep to these rules, and one draw needn't show every extreme that they name: The counts sum to 22528; the captions of image m are the consecutive rows start[m] to start[m] + sentences_for_picture[m] - 1 of sentence_encoder_result, where start[m] is the sum of the counts of images before m; some image has 8.
All inputs are finite; a program needn't handle non-finite values.
Results may differ from a plain program's by a relative error of at most 0.014.
Values may be sent and summed in bfloat16 or wider, within the bound.
A program may use at most 64 MiB of HBM per device.

v0:
```python
import jax
import jax.numpy as jnp
from jax import lax
from jax.sharding import PartitionSpec as P

epsilon = 1e-06


def passed_along(value, axis, steps):
    count = lax.axis_size(axis)
    pairs = [(source, (source + steps) % count) for source in range(count)]
    return lax.ppermute(value, axis, pairs)


def embed(features, loss_multiplier):
    raw = jnp.dot(features, loss_multiplier, preferred_element_type=jnp.float32)
    scale = lax.rsqrt(jnp.sum(raw * raw, axis=1, keepdims=True) + epsilon)
    return (raw * scale, scale)


def scaling_factor(
    similarity_matrix,
    other_begin_list,
    sentence_tally_later,
    other_position,
    scaled_sharpness,
    displacement,
):
    raw_similarity = scaled_sharpness * similarity_matrix + displacement
    inside = (other_position >= other_begin_list) & (
        other_position < other_begin_list + sentence_tally_later
    )
    match_polarity = jnp.where(inside, 1.0, -1.0)
    loss_multiplier = jnp.where(inside, 1.0 / sentence_tally_later.astype(jnp.float32), 1.0)
    return (
        scaled_sharpness
        * (-match_polarity * loss_multiplier * jax.nn.sigmoid(-match_polarity * raw_similarity))
    ).astype(jnp.bfloat16)


def unit_back(grad, unit, scale):
    return scale * (grad - unit * jnp.sum(unit * grad, axis=1, keepdims=True))


def divided_product(values, loss_multiplier):
    upper = lax.optimization_barrier(values.astype(jnp.bfloat16))
    lower = (values - upper.astype(jnp.float32)).astype(jnp.bfloat16)
    first = jnp.einsum("me,de->md", upper, loss_multiplier, preferred_element_type=jnp.float32)
    return first + jnp.einsum(
        "me,de->md", lower, loss_multiplier, preferred_element_type=jnp.float32
    )


def body(
    picture_encoder_result,
    sentence_encoder_result,
    picture_projector_matrix,
    sentence_projector_matrix,
    sentences_for_picture,
    sharpness_factor,
    score_offset_term,
):
    full_img, full_cap = (
        lax.all_gather(picture_projector_matrix, "tensor", axis=1, tiled=True),
        lax.all_gather(sentence_projector_matrix, "tensor", axis=1, tiled=True),
    )
    img_unit, img_scale = embed(picture_encoder_result, full_img)
    cap_unit, cap_scale = embed(sentence_encoder_result, full_cap)
    img_z = img_unit.astype(jnp.bfloat16)
    cap_z = cap_unit.astype(jnp.bfloat16)
    scaled_sharpness = sharpness_factor[0]
    displacement = score_offset_term[0]
    ends = jnp.cumsum(sentences_for_picture)
    starts = ends - sentences_for_picture
    cycle_count = lax.axis_size("dp")
    tensor_count = lax.axis_size("tensor")
    cycle_pos = lax.axis_index("dp")
    tensor_pos = lax.axis_index("tensor")
    img_rows = picture_encoder_result.shape[0]
    cap_rows = sentence_encoder_result.shape[0]
    width = img_z.shape[1]
    row_iota = jnp.arange(cap_rows, dtype=jnp.int32)
    sentence_number = (cycle_pos * tensor_count + tensor_pos) * cap_rows + row_iota

    def block_of(anchor):
        first = anchor * img_rows
        group_begin_list = lax.dynamic_slice_in_dim(starts, first, img_rows)
        group_sizes_list = lax.dynamic_slice_in_dim(sentences_for_picture, first, img_rows)
        return (group_begin_list, group_sizes_list)

    def image_tile(block_z, anchor):
        group_begin_list, group_sizes_list = block_of(anchor)
        similarity_matrix = jnp.einsum(
            "me,ce->mc", block_z, cap_z, preferred_element_type=jnp.float32
        )
        return scaling_factor(
            similarity_matrix,
            group_begin_list[:, None],
            group_sizes_list[:, None],
            sentence_number[None, :],
            scaled_sharpness,
            displacement,
        )

    def step(turn, state):
        block_z, carried, cap_grad = state
        anchor = (cycle_pos - turn) % cycle_count
        pair_factor = image_tile(block_z, anchor)
        cap_grad = cap_grad + jnp.einsum(
            "mc,me->ce", pair_factor, block_z, preferred_element_type=jnp.float32
        )
        carried = carried + jnp.dot(pair_factor, cap_z, preferred_element_type=jnp.float32)
        carried = passed_along(carried.astype(jnp.bfloat16), "dp", 1).astype(carried.dtype)
        block_z = passed_along(block_z, "dp", 1)
        return (block_z, carried, cap_grad)

    start_state = (
        img_z,
        jnp.zeros((img_rows, width), jnp.float32),
        jnp.zeros((cap_rows, width), jnp.float32),
    )
    unused, img_grad, cap_grad = lax.fori_loop(0, cycle_count, step, start_state)
    img_back = unit_back(img_grad, img_unit, img_scale)
    img_part = divided_product(img_back, full_img)
    grad_img = lax.psum_scatter(
        img_part.astype(jnp.bfloat16), "tensor", scatter_dimension=1, tiled=True
    )
    cap_back = unit_back(cap_grad, cap_unit, cap_scale)
    grad_cap = divided_product(cap_back, full_cap)
    return (grad_img, grad_cap.astype(jnp.bfloat16))


def solution(mesh):
    in_specs = (
        P("dp", None),
        P(("dp", "tensor"), None),
        P(None, "tensor"),
        P(None, "tensor"),
        P(),
        P(),
        P(),
    )
    out_specs = (P("dp", "tensor"), P(("dp", "tensor"), None))
    return jax.shard_map(body, mesh=mesh, in_specs=in_specs, out_specs=out_specs, check_vma=False)
```

profile of v0, /device:TPU:0, one launch (start us, length us, event | category | flops | bytes accessed | tf_op | source)
XLA Modules:
  0.0 632.3 jit_solution(152464883537165580)
XLA Ops:
  10.8 56.4 %all-gather.5.cloned.1.call-done = bf16[1024,1024]{1,0:T(8,128)(2,1)} async-done(((bf16[1024,128]{1,0:T(8,128)(2,1)}), bf16[1024,1024]{1,0:T(8,128)(2,1)}) %all-gather.5.cloned.1.call-update) | async-done | bytes 2097168 | tf_op jit(solution)/shard_map/all_gather | solution.py:65
  67.3 2.4 multiply_reduce_fusion.3
  69.7 52.2 %all-gather.3.cloned.1.call-done = bf16[1024,1024]{1,0:T(8,128)(2,1)} async-done(((bf16[1024,128]{1,0:T(8,128)(2,1)}), bf16[1024,1024]{1,0:T(8,128)(2,1)}) %all-gather.3.cloned.1.call-update) | async-done | bytes 2097168 | tf_op jit(solution)/shard_map/all_gather | solution.py:64
  121.9 2.6 multiply_reduce_fusion.1
  125.9 424.6 %while.20 = (s32[]{:T(128)}, bf16[352,1024]{1,0:T(8,128)(2,1)}, f32[352,1024]{1,0:T(8,128)S(1)}, f32[176,1024]{1,0:T(8,128)}, f32[]{:T(128)}, /*index=5*/s32[]{:...) while((s32[]{:T(128)}, bf16[352,1024]{1,0:T(8,128)(2,1)}, ...), condition=%wide.region_5.6_spmd.clone, body=%wide.region_4.5_spmd.clone.sunk | while | flops 383427808 | bytes 15525043 | solution.py:122
  128.5 1.8 fusion.48
  134.4 10.3 %collective-permute-done.1 = bf16[352,1024]{1,0:T(8,128)(2,1)} collective-permute-done((bf16[352,1024]{1,0:T(8,128)(2,1)}, bf16[352,1024]{1,0:T(8,128)(2,1)}, u32[]{:S(2)}, u32[]{:S(2)}) %collective-permute-start.1) | collective-permute-done | bytes 720928 | tf_op jit(solution)/shard_map/while/body/eval_jaxpr/ppermute | solution.py:12
  146.0 6.5 %collective-permute-done = bf16[352,1024]{1,0:T(8,128)(2,1)} collective-permute-done((bf16[352,1024]{1,0:T(8,128)(2,1)S(1)}, bf16[352,1024]{1,0:T(8,128)(2,1)}, u32[]{:S(2)}, u32[]{:S(2)}) %collective-permute-start) | collective-permute-done | bytes 720928 | tf_op jit(solution)/shard_map/while/body/eval_jaxpr/ppermute | solution.py:12
  155.1 1.8 fusion.48
  158.1 2.3 convolution_add_fusion.5
  160.4 10.8 %collective-permute-done.1 = bf16[352,1024]{1,0:T(8,128)(2,1)} collective-permute-done((bf16[352,1024]{1,0:T(8,128)(2,1)}, bf16[352,1024]{1,0:T(8,128)(2,1)}, u32[]{:S(2)}, u32[]{:S(2)}) %collective-permute-start.1) | collective-permute-done | bytes 720928 | tf_op jit(solution)/shard_map/while/body/eval_jaxpr/ppermute | solution.py:12
  172.5 6.5 %collective-permute-done = bf16[352,1024]{1,0:T(8,128)(2,1)} collective-permute-done((bf16[352,1024]{1,0:T(8,128)(2,1)S(1)}, bf16[352,1024]{1,0:T(8,128)(2,1)}, u32[]{:S(2)}, u32[]{:S(2)}) %collective-permute-start) | collective-permute-done | bytes 720928 | tf_op jit(solution)/shard_map/while/body/eval_jaxpr/ppermute | solution.py:12
  181.6 1.8 fusion.48
  184.6 2.3 convolution_add_fusion.5
  187.0 10.8 %collective-permute-done.1 = bf16[352,1024]{1,0:T(8,128)(2,1)} collective-permute-done((bf16[352,1024]{1,0:T(8,128)(2,1)}, bf16[352,1024]{1,0:T(8,128)(2,1)}, u32[]{:S(2)}, u32[]{:S(2)}) %collective-permute-start.1) | collective-permute-done | bytes 720928 | tf_op jit(solution)/shard_map/while/body/eval_jaxpr/ppermute | solution.py:12
  199.0 6.5 %collective-permute-done = bf16[352,1024]{1,0:T(8,128)(2,1)} collective-permute-done((bf16[352,1024]{1,0:T(8,128)(2,1)S(1)}, bf16[352,1024]{1,0:T(8,128)(2,1)}, u32[]{:S(2)}, u32[]{:S(2)}) %collective-permute-start) | collective-permute-done | bytes 720928 | tf_op jit(solution)/shard_map/while/body/eval_jaxpr/ppermute | solution.py:12
  208.2 1.8 fusion.48
  211.2 2.3 convolution_add_fusion.5
  213.5 10.8 %collective-permute-done.1 = bf16[352,1024]{1,0:T(8,128)(2,1)} collective-permute-done((bf16[352,1024]{1,0:T(8,128)(2,1)}, bf16[352,1024]{1,0:T(8,128)(2,1)}, u32[]{:S(2)}, u32[]{:S(2)}) %collective-permute-start.1) | collective-permute-done | bytes 720928 | tf_op jit(solution)/shard_map/while/body/eval_jaxpr/ppermute | solution.py:12
  225.6 6.5 %collective-permute-done = bf16[352,1024]{1,0:T(8,128)(2,1)} collective-permute-done((bf16[352,1024]{1,0:T(8,128)(2,1)S(1)}, bf16[352,1024]{1,0:T(8,128)(2,1)}, u32[]{:S(2)}, u32[]{:S(2)}) %collective-permute-start) | collective-permute-done | bytes 720928 | tf_op jit(solution)/shard_map/while/body/eval_jaxpr/ppermute | solution.py:12
  237.7 2.3 convolution_add_fusion.5
  240.1 10.8 %collective-permute-done.1 = bf16[352,1024]{1,0:T(8,128)(2,1)} collective-permute-done((bf16[352,1024]{1,0:T(8,128)(2,1)}, bf16[352,1024]{1,0:T(8,128)(2,1)}, u32[]{:S(2)}, u32[]{:S(2)}) %collective-permute-start.1) | collective-permute-done | bytes 720928 | tf_op jit(solution)/shard_map/while/body/eval_jaxpr/ppermute | solution.py:12
  252.1 6.5 %collective-permute-done = bf16[352,1024]{1,0:T(8,128)(2,1)} collective-permute-done((bf16[352,1024]{1,0:T(8,128)(2,1)S(1)}, bf16[352,1024]{1,0:T(8,128)(2,1)}, u32[]{:S(2)}, u32[]{:S(2)}) %collective-permute-start) | collective-permute-done | bytes 720928 | tf_op jit(solution)/shard_map/while/body/eval_jaxpr/ppermute | solution.py:12
  261.2 1.8 fusion.48
  264.2 2.3 convolution_add_fusion.5
  266.6 10.8 %collective-permute-done.1 = bf16[352,1024]{1,0:T(8,128)(2,1)} collective-permute-done((bf16[352,1024]{1,0:T(8,128)(2,1)}, bf16[352,1024]{1,0:T(8,128)(2,1)}, u32[]{:S(2)}, u32[]{:S(2)}) %collective-permute-start.1) | collective-permute-done | bytes 720928 | tf_op jit(solution)/shard_map/while/body/eval_jaxpr/ppermute | solution.py:12
  278.6 6.5 %collective-permute-done = bf16[352,1024]{1,0:T(8,128)(2,1)} collective-permute-done((bf16[352,1024]{1,0:T(8,128)(2,1)S(1)}, bf16[352,1024]{1,0:T(8,128)(2,1)}, u32[]{:S(2)}, u32[]{:S(2)}) %collective-permute-start) | collective-permute-done | bytes 720928 | tf_op jit(solution)/shard_map/while/body/eval_jaxpr/ppermute | solution.py:12
  287.8 1.8 fusion.48
  290.8 2.3 convolution_add_fusion.5
  293.1 10.8 %collective-permute-done.1 = bf16[352,1024]{1,0:T(8,128)(2,1)} collective-permute-done((bf16[352,1024]{1,0:T(8,128)(2,1)}, bf16[352,1024]{1,0:T(8,128)(2,1)}, u32[]{:S(2)}, u32[]{:S(2)}) %collective-permute-start.1) | collective-permute-done | bytes 720928 | tf_op jit(solution)/shard_map/while/body/eval_jaxpr/ppermute | solution.py:12
  305.2 6.5 %collective-permute-done = bf16[352,1024]{1,0:T(8,128)(2,1)} collective-permute-done((bf16[352,1024]{1,0:T(8,128)(2,1)S(1)}, bf16[352,1024]{1,0:T(8,128)(2,1)}, u32[]{:S(2)}, u32[]{:S(2)}) %collective-permute-start) | collective-permute-done | bytes 720928 | tf_op jit(solution)/shard_map/while/body/eval_jaxpr/ppermute | solution.py:12
  317.3 2.3 convolution_add_fusion.5
  319.7 10.8 %collective-permute-done.1 = bf16[352,1024]{1,0:T(8,128)(2,1)} collective-permute-done((bf16[352,1024]{1,0:T(8,128)(2,1)}, bf16[352,1024]{1,0:T(8,128)(2,1)}, u32[]{:S(2)}, u32[]{:S(2)}) %collective-permute-start.1) | collective-permute-done | bytes 720928 | tf_op jit(solution)/shard_map/while/body/eval_jaxpr/ppermute | solution.py:12
  331.7 6.5 %collective-permute-done = bf16[352,1024]{1,0:T(8,128)(2,1)} collective-permute-done((bf16[352,1024]{1,0:T(8,128)(2,1)S(1)}, bf16[352,1024]{1,0:T(8,128)(2,1)}, u32[]{:S(2)}, u32[]{:S(2)}) %collective-permute-start) | collective-permute-done | bytes 720928 | tf_op jit(solution)/shard_map/while/body/eval_jaxpr/ppermute | solution.py:12
  340.9 1.8 fusion.48
  343.9 2.3 convolution_add_fusion.5
  346.2 10.8 %collective-permute-done.1 = bf16[352,1024]{1,0:T(8,128)(2,1)} collective-permute-done((bf16[352,1024]{1,0:T(8,128)(2,1)}, bf16[352,1024]{1,0:T(8,128)(2,1)}, u32[]{:S(2)}, u32[]{:S(2)}) %collective-permute-start.1) | collective-permute-done | bytes 720928 | tf_op jit(solution)/shard_map/while/body/eval_jaxpr/ppermute | solution.py:12
  358.3 6.5 %collective-permute-done = bf16[352,1024]{1,0:T(8,128)(2,1)} collective-permute-done((bf16[352,1024]{1,0:T(8,128)(2,1)S(1)}, bf16[352,1024]{1,0:T(8,128)(2,1)}, u32[]{:S(2)}, u32[]{:S(2)}) %collective-permute-start) | collective-permute-done | bytes 720928 | tf_op jit(solution)/shard_map/while/body/eval_jaxpr/ppermute | solution.py:12
  367.4 1.8 fusion.48
  370.4 2.3 convolution_add_fusion.5
  372.7 10.8 %collective-permute-done.1 = bf16[352,1024]{1,0:T(8,128)(2,1)} collective-permute-done((bf16[352,1024]{1,0:T(8,128)(2,1)}, bf16[352,1024]{1,0:T(8,128)(2,1)}, u32[]{:S(2)}, u32[]{:S(2)}) %collective-permute-start.1) | collective-permute-done | bytes 720928 | tf_op jit(solution)/shard_map/while/body/eval_jaxpr/ppermute | solution.py:12
  384.8 6.5 %collective-permute-done = bf16[352,1024]{1,0:T(8,128)(2,1)} collective-permute-done((bf16[352,1024]{1,0:T(8,128)(2,1)S(1)}, bf16[352,1024]{1,0:T(8,128)(2,1)}, u32[]{:S(2)}, u32[]{:S(2)}) %collective-permute-start) | collective-permute-done | bytes 720928 | tf_op jit(solution)/shard_map/while/body/eval_jaxpr/ppermute | solution.py:12
  393.9 1.8 fusion.48
  397.0 2.3 convolution_add_fusion.5
  399.3 10.8 %collective-permute-done.1 = bf16[352,1024]{1,0:T(8,128)(2,1)} collective-permute-done((bf16[352,1024]{1,0:T(8,128)(2,1)}, bf16[352,1024]{1,0:T(8,128)(2,1)}, u32[]{:S(2)}, u32[]{:S(2)}) %collective-permute-start.1) | collective-permute-done | bytes 720928 | tf_op jit(solution)/shard_map/while/body/eval_jaxpr/ppermute | solution.py:12
  411.4 6.5 %collective-permute-done = bf16[352,1024]{1,0:T(8,128)(2,1)} collective-permute-done((bf16[352,1024]{1,0:T(8,128)(2,1)S(1)}, bf16[352,1024]{1,0:T(8,128)(2,1)}, u32[]{:S(2)}, u32[]{:S(2)}) %collective-permute-start) | collective-permute-done | bytes 720928 | tf_op jit(solution)/shard_map/while/body/eval_jaxpr/ppermute | solution.py:12
  423.5 2.3 convolution_add_fusion.5
  425.8 10.8 %collective-permute-done.1 = bf16[352,1024]{1,0:T(8,128)(2,1)} collective-permute-done((bf16[352,1024]{1,0:T(8,128)(2,1)}, bf16[352,1024]{1,0:T(8,128)(2,1)}, u32[]{:S(2)}, u32[]{:S(2)}) %collective-permute-start.1) | collective-permute-done | bytes 720928 | tf_op jit(solution)/shard_map/while/body/eval_jaxpr/ppermute | solution.py:12
  437.9 6.5 %collective-permute-done = bf16[352,1024]{1,0:T(8,128)(2,1)} collective-permute-done((bf16[352,1024]{1,0:T(8,128)(2,1)S(1)}, bf16[352,1024]{1,0:T(8,128)(2,1)}, u32[]{:S(2)}, u32[]{:S(2)}) %collective-permute-start) | collective-permute-done | bytes 720928 | tf_op jit(solution)/shard_map/while/body/eval_jaxpr/ppermute | solution.py:12
  447.0 1.8 fusion.48
  450.0 2.3 convolution_add_fusion.5
  452.4 10.8 %collective-permute-done.1 = bf16[352,1024]{1,0:T(8,128)(2,1)} collective-permute-done((bf16[352,1024]{1,0:T(8,128)(2,1)}, bf16[352,1024]{1,0:T(8,128)(2,1)}, u32[]{:S(2)}, u32[]{:S(2)}) %collective-permute-start.1) | collective-permute-done | bytes 720928 | tf_op jit(solution)/shard_map/while/body/eval_jaxpr/ppermute | solution.py:12
  464.4 6.5 %collective-permute-done = bf16[352,1024]{1,0:T(8,128)(2,1)} collective-permute-done((bf16[352,1024]{1,0:T(8,128)(2,1)S(1)}, bf16[352,1024]{1,0:T(8,128)(2,1)}, u32[]{:S(2)}, u32[]{:S(2)}) %collective-permute-start) | collective-permute-done | bytes 720928 | tf_op jit(solution)/shard_map/while/body/eval_jaxpr/ppermute | solution.py:12
  473.6 1.8 fusion.48
  476.6 2.3 convolution_add_fusion.5
  478.9 10.8 %collective-permute-done.1 = bf16[352,1024]{1,0:T(8,128)(2,1)} collective-permute-done((bf16[352,1024]{1,0:T(8,128)(2,1)}, bf16[352,1024]{1,0:T(8,128)(2,1)}, u32[]{:S(2)}, u32[]{:S(2)}) %collective-permute-start.1) | collective-permute-done | bytes 720928 | tf_op jit(solution)/shard_map/while/body/eval_jaxpr/ppermute | solution.py:12
  491.0 6.5 %collective-permute-done = bf16[352,1024]{1,0:T(8,128)(2,1)} collective-permute-done((bf16[352,1024]{1,0:T(8,128)(2,1)S(1)}, bf16[352,1024]{1,0:T(8,128)(2,1)}, u32[]{:S(2)}, u32[]{:S(2)}) %collective-permute-start) | collective-permute-done | bytes 720928 | tf_op jit(solution)/shard_map/while/body/eval_jaxpr/ppermute | solution.py:12
  503.1 2.3 convolution_add_fusion.5
  505.5 10.8 %collective-permute-done.1 = bf16[352,1024]{1,0:T(8,128)(2,1)} collective-permute-done((bf16[352,1024]{1,0:T(8,128)(2,1)}, bf16[352,1024]{1,0:T(8,128)(2,1)}, u32[]{:S(2)}, u32[]{:S(2)}) %collective-permute-start.1) | collective-permute-done | bytes 720928 | tf_op jit(solution)/shard_map/while/body/eval_jaxpr/ppermute | solution.py:12
  517.5 6.5 %collective-permute-done = bf16[352,1024]{1,0:T(8,128)(2,1)} collective-permute-done((bf16[352,1024]{1,0:T(8,128)(2,1)S(1)}, bf16[352,1024]{1,0:T(8,128)(2,1)}, u32[]{:S(2)}, u32[]{:S(2)}) %collective-permute-start) | collective-permute-done | bytes 720928 | tf_op jit(solution)/shard_map/while/body/eval_jaxpr/ppermute | solution.py:12
  529.7 2.3 convolution_add_fusion.5
  532.0 10.8 %collective-permute-done.1 = bf16[352,1024]{1,0:T(8,128)(2,1)} collective-permute-done((bf16[352,1024]{1,0:T(8,128)(2,1)}, bf16[352,1024]{1,0:T(8,128)(2,1)}, u32[]{:S(2)}, u32[]{:S(2)}) %collective-permute-start.1) | collective-permute-done | bytes 720928 | tf_op jit(solution)/shard_map/while/body/eval_jaxpr/ppermute | solution.py:12
  544.1 6.5 %collective-permute-done = bf16[352,1024]{1,0:T(8,128)(2,1)} collective-permute-done((bf16[352,1024]{1,0:T(8,128)(2,1)S(1)}, bf16[352,1024]{1,0:T(8,128)(2,1)}, u32[]{:S(2)}, u32[]{:S(2)}) %collective-permute-start) | collective-permute-done | bytes 720928 | tf_op jit(solution)/shard_map/while/body/eval_jaxpr/ppermute | solution.py:12
  561.6 62.6 %reduce-scatter.4.cloned.1.call-done = bf16[128,352]{1,0:T(8,128)(2,1)} async-done(((bf16[1024,352]{1,0:T(8,128)(2,1)}), bf16[128,352]{1,0:T(8,128)(2,1)}) %reduce-scatter.4.cloned.1.call-update) | async-done | bytes 90128
  (177 shorter events, 111.9 us)
Async XLA Ops:
  7.2 114.7 %copy-start = (bf16[352,1024]{1,0:T(8,128)(2,1)S(1)}, bf16[352,1024]{1,0:T(8,128)(2,1)}, u32[]{:S(2)}) copy-start(bf16[352,1024]{1,0:T(8,128)(2,1)} %param.9) | copy-start | bytes 2162692
  7.2 60.1 %all-gather.5.cloned.1.call-start = ((), (), s32[]{:S(2)}) async-start(), calls=%async_computation.2 | async-start | bytes 2359296 | tf_op jit(solution)/shard_map/all_gather | solution.py:65
  7.9 113.9 %all-gather.3.cloned.1.call-start = ((), (), s32[]{:S(2)}) async-start(), calls=%async_computation.1 | async-start | bytes 2359296 | tf_op jit(solution)/shard_map/all_gather | solution.py:64
  8.7 615.5 %reduce-scatter.4.cloned.1.call-start = ((), (), s32[]{:S(2)}) async-start(), calls=%async_computation.3 | async-start | bytes 884736
  69.7 54.8 %copy-start.5 = (f32[176,1024]{1,0:T(8,128)}, f32[176,1024]{1,0:T(8,128)S(1)}, u32[]{:S(2)}) copy-start(f32[176,1024]{1,0:T(8,128)S(1)} %get-tuple-element.336) | copy-start | bytes 2162692
  124.5 1.4 copy-start.2
  131.6 13.1 %collective-permute-start.1 = (bf16[352,1024]{1,0:T(8,128)(2,1)}, bf16[352,1024]{1,0:T(8,128)(2,1)}, u32[]{:S(2)}, u32[]{:S(2)}) collective-permute-start(bf16[352,1024]{1,0:T(8,128)(2,1)} %fusion.49), channel_id=1, source_target_pairs={{0,8},{8,16},{16,24},{24,32},{32,40},{40,48},{48,56},{56,64},{64,7... | collective-permute-start | bytes 2162696 | tf_op jit(solution)/shard_map/while/body/eval_jaxpr/ppermute | solution.py:12
  131.6 20.9 %collective-permute-start = (bf16[352,1024]{1,0:T(8,128)(2,1)S(1)}, bf16[352,1024]{1,0:T(8,128)(2,1)}, u32[]{:S(2)}, u32[]{:S(2)}) collective-permute-start(bf16[352,1024]{1,0:T(8,128)(2,1)S(1)} %copy.16), channel_id=1, source_target_pairs={{0,8},{8,16},{16,24},{24,32},{32,40},{40,48},{48,56},{56,64},{64,7... | collective-permute-start | bytes 2162696 | tf_op jit(solution)/shard_map/while/body/eval_jaxpr/ppermute | solution.py:12
  158.1 13.1 %collective-permute-start.1 = (bf16[352,1024]{1,0:T(8,128)(2,1)}, bf16[352,1024]{1,0:T(8,128)(2,1)}, u32[]{:S(2)}, u32[]{:S(2)}) collective-permute-start(bf16[352,1024]{1,0:T(8,128)(2,1)} %fusion.49), channel_id=1, source_target_pairs={{0,8},{8,16},{16,24},{24,32},{32,40},{40,48},{48,56},{56,64},{64,7... | collective-permute-start | bytes 2162696 | tf_op jit(solution)/shard_map/while/body/eval_jaxpr/ppermute | solution.py:12
  158.1 20.9 %collective-permute-start = (bf16[352,1024]{1,0:T(8,128)(2,1)S(1)}, bf16[352,1024]{1,0:T(8,128)(2,1)}, u32[]{:S(2)}, u32[]{:S(2)}) collective-permute-start(bf16[352,1024]{1,0:T(8,128)(2,1)S(1)} %copy.16), channel_id=1, source_target_pairs={{0,8},{8,16},{16,24},{24,32},{32,40},{40,48},{48,56},{56,64},{64,7... | collective-permute-start | bytes 2162696 | tf_op jit(solution)/shard_map/while/body/eval_jaxpr/ppermute | solution.py:12
  184.6 13.1 %collective-permute-start.1 = (bf16[352,1024]{1,0:T(8,128)(2,1)}, bf16[352,1024]{1,0:T(8,128)(2,1)}, u32[]{:S(2)}, u32[]{:S(2)}) collective-permute-start(bf16[352,1024]{1,0:T(8,128)(2,1)} %fusion.49), channel_id=1, source_target_pairs={{0,8},{8,16},{16,24},{24,32},{32,40},{40,48},{48,56},{56,64},{64,7... | collective-permute-start | bytes 2162696 | tf_op jit(solution)/shard_map/while/body/eval_jaxpr/ppermute | solution.py:12
  184.6 20.9 %collective-permute-start = (bf16[352,1024]{1,0:T(8,128)(2,1)S(1)}, bf16[352,1024]{1,0:T(8,128)(2,1)}, u32[]{:S(2)}, u32[]{:S(2)}) collective-permute-start(bf16[352,1024]{1,0:T(8,128)(2,1)S(1)} %copy.16), channel_id=1, source_target_pairs={{0,8},{8,16},{16,24},{24,32},{32,40},{40,48},{48,56},{56,64},{64,7... | collective-permute-start | bytes 2162696 | tf_op jit(solution)/shard_map/while/body/eval_jaxpr/ppermute | solution.py:12
  211.2 13.1 %collective-permute-start.1 = (bf16[352,1024]{1,0:T(8,128)(2,1)}, bf16[352,1024]{1,0:T(8,128)(2,1)}, u32[]{:S(2)}, u32[]{:S(2)}) collective-permute-start(bf16[352,1024]{1,0:T(8,128)(2,1)} %fusion.49), channel_id=1, source_target_pairs={{0,8},{8,16},{16,24},{24,32},{32,40},{40,48},{48,56},{56,64},{64,7... | collective-permute-start | bytes 2162696 | tf_op jit(solution)/shard_map/while/body/eval_jaxpr/ppermute | solution.py:12
  211.2 20.9 %collective-permute-start = (bf16[352,1024]{1,0:T(8,128)(2,1)S(1)}, bf16[352,1024]{1,0:T(8,128)(2,1)}, u32[]{:S(2)}, u32[]{:S(2)}) collective-permute-start(bf16[352,1024]{1,0:T(8,128)(2,1)S(1)} %copy.16), channel_id=1, source_target_pairs={{0,8},{8,16},{16,24},{24,32},{32,40},{40,48},{48,56},{56,64},{64,7... | collective-permute-start | bytes 2162696 | tf_op jit(solution)/shard_map/while/body/eval_jaxpr/ppermute | solution.py:12
  237.7 13.1 %collective-permute-start.1 = (bf16[352,1024]{1,0:T(8,128)(2,1)}, bf16[352,1024]{1,0:T(8,128)(2,1)}, u32[]{:S(2)}, u32[]{:S(2)}) collective-permute-start(bf16[352,1024]{1,0:T(8,128)(2,1)} %fusion.49), channel_id=1, source_target_pairs={{0,8},{8,16},{16,24},{24,32},{32,40},{40,48},{48,56},{56,64},{64,7... | collective-permute-start | bytes 2162696 | tf_op jit(solution)/shard_map/while/body/eval_jaxpr/ppermute | solution.py:12
  237.7 20.9 %collective-permute-start = (bf16[352,1024]{1,0:T(8,128)(2,1)S(1)}, bf16[352,1024]{1,0:T(8,128)(2,1)}, u32[]{:S(2)}, u32[]{:S(2)}) collective-permute-start(bf16[352,1024]{1,0:T(8,128)(2,1)S(1)} %copy.16), channel_id=1, source_target_pairs={{0,8},{8,16},{16,24},{24,32},{32,40},{40,48},{48,56},{56,64},{64,7... | collective-permute-start | bytes 2162696 | tf_op jit(solution)/shard_map/while/body/eval_jaxpr/ppermute | solution.py:12
  264.2 13.1 %collective-permute-start.1 = (bf16[352,1024]{1,0:T(8,128)(2,1)}, bf16[352,1024]{1,0:T(8,128)(2,1)}, u32[]{:S(2)}, u32[]{:S(2)}) collective-permute-start(bf16[352,1024]{1,0:T(8,128)(2,1)} %fusion.49), channel_id=1, source_target_pairs={{0,8},{8,16},{16,24},{24,32},{32,40},{40,48},{48,56},{56,64},{64,7... | collective-permute-start | bytes 2162696 | tf_op jit(solution)/shard_map/while/body/eval_jaxpr/ppermute | solution.py:12
  264.2 20.9 %collective-permute-start = (bf16[352,1024]{1,0:T(8,128)(2,1)S(1)}, bf16[352,1024]{1,0:T(8,128)(2,1)}, u32[]{:S(2)}, u32[]{:S(2)}) collective-permute-start(bf16[352,1024]{1,0:T(8,128)(2,1)S(1)} %copy.16), channel_id=1, source_target_pairs={{0,8},{8,16},{16,24},{24,32},{32,40},{40,48},{48,56},{56,64},{64,7... | collective-permute-start | bytes 2162696 | tf_op jit(solution)/shard_map/while/body/eval_jaxpr/ppermute | solution.py:12
  290.8 13.1 %collective-permute-start.1 = (bf16[352,1024]{1,0:T(8,128)(2,1)}, bf16[352,1024]{1,0:T(8,128)(2,1)}, u32[]{:S(2)}, u32[]{:S(2)}) collective-permute-start(bf16[352,1024]{1,0:T(8,128)(2,1)} %fusion.49), channel_id=1, source_target_pairs={{0,8},{8,16},{16,24},{24,32},{32,40},{40,48},{48,56},{56,64},{64,7... | collective-permute-start | bytes 2162696 | tf_op jit(solution)/shard_map/while/body/eval_jaxpr/ppermute | solution.py:12
  290.8 20.9 %collective-permute-start = (bf16[352,1024]{1,0:T(8,128)(2,1)S(1)}, bf16[352,1024]{1,0:T(8,128)(2,1)}, u32[]{:S(2)}, u32[]{:S(2)}) collective-permute-start(bf16[352,1024]{1,0:T(8,128)(2,1)S(1)} %copy.16), channel_id=1, source_target_pairs={{0,8},{8,16},{16,24},{24,32},{32,40},{40,48},{48,56},{56,64},{64,7... | collective-permute-start | bytes 2162696 | tf_op jit(solution)/shard_map/while/body/eval_jaxpr/ppermute | solution.py:12
  317.3 13.1 %collective-permute-start.1 = (bf16[352,1024]{1,0:T(8,128)(2,1)}, bf16[352,1024]{1,0:T(8,128)(2,1)}, u32[]{:S(2)}, u32[]{:S(2)}) collective-permute-start(bf16[352,1024]{1,0:T(8,128)(2,1)} %fusion.49), channel_id=1, source_target_pairs={{0,8},{8,16},{16,24},{24,32},{32,40},{40,48},{48,56},{56,64},{64,7... | collective-permute-start | bytes 2162696 | tf_op jit(solution)/shard_map/while/body/eval_jaxpr/ppermute | solution.py:12
  317.3 20.9 %collective-permute-start = (bf16[352,1024]{1,0:T(8,128)(2,1)S(1)}, bf16[352,1024]{1,0:T(8,128)(2,1)}, u32[]{:S(2)}, u32[]{:S(2)}) collective-permute-start(bf16[352,1024]{1,0:T(8,128)(2,1)S(1)} %copy.16), channel_id=1, source_target_pairs={{0,8},{8,16},{16,24},{24,32},{32,40},{40,48},{48,56},{56,64},{64,7... | collective-permute-start | bytes 2162696 | tf_op jit(solution)/shard_map/while/body/eval_jaxpr/ppermute | solution.py:12
  343.9 13.1 %collective-permute-start.1 = (bf16[352,1024]{1,0:T(8,128)(2,1)}, bf16[352,1024]{1,0:T(8,128)(2,1)}, u32[]{:S(2)}, u32[]{:S(2)}) collective-permute-start(bf16[352,1024]{1,0:T(8,128)(2,1)} %fusion.49), channel_id=1, source_target_pairs={{0,8},{8,16},{16,24},{24,32},{32,40},{40,48},{48,56},{56,64},{64,7... | collective-permute-start | bytes 2162696 | tf_op jit(solution)/shard_map/while/body/eval_jaxpr/ppermute | solution.py:12
  343.9 20.9 %collective-permute-start = (bf16[352,1024]{1,0:T(8,128)(2,1)S(1)}, bf16[352,1024]{1,0:T(8,128)(2,1)}, u32[]{:S(2)}, u32[]{:S(2)}) collective-permute-start(bf16[352,1024]{1,0:T(8,128)(2,1)S(1)} %copy.16), channel_id=1, source_target_pairs={{0,8},{8,16},{16,24},{24,32},{32,40},{40,48},{48,56},{56,64},{64,7... | collective-permute-start | bytes 2162696 | tf_op jit(solution)/shard_map/while/body/eval_jaxpr/ppermute | solution.py:12
  370.4 13.1 %collective-permute-start.1 = (bf16[352,1024]{1,0:T(8,128)(2,1)}, bf16[352,1024]{1,0:T(8,128)(2,1)}, u32[]{:S(2)}, u32[]{:S(2)}) collective-permute-start(bf16[352,1024]{1,0:T(8,128)(2,1)} %fusion.49), channel_id=1, source_target_pairs={{0,8},{8,16},{16,24},{24,32},{32,40},{40,48},{48,56},{56,64},{64,7... | collective-permute-start | bytes 2162696 | tf_op jit(solution)/shard_map/while/body/eval_jaxpr/ppermute | solution.py:12
  370.4 20.9 %collective-permute-start = (bf16[352,1024]{1,0:T(8,128)(2,1)S(1)}, bf16[352,1024]{1,0:T(8,128)(2,1)}, u32[]{:S(2)}, u32[]{:S(2)}) collective-permute-start(bf16[352,1024]{1,0:T(8,128)(2,1)S(1)} %copy.16), channel_id=1, source_target_pairs={{0,8},{8,16},{16,24},{24,32},{32,40},{40,48},{48,56},{56,64},{64,7... | collective-permute-start | bytes 2162696 | tf_op jit(solution)/shard_map/while/body/eval_jaxpr/ppermute | solution.py:12
  396.9 13.1 %collective-permute-start.1 = (bf16[352,1024]{1,0:T(8,128)(2,1)}, bf16[352,1024]{1,0:T(8,128)(2,1)}, u32[]{:S(2)}, u32[]{:S(2)}) collective-permute-start(bf16[352,1024]{1,0:T(8,128)(2,1)} %fusion.49), channel_id=1, source_target_pairs={{0,8},{8,16},{16,24},{24,32},{32,40},{40,48},{48,56},{56,64},{64,7... | collective-permute-start | bytes 2162696 | tf_op jit(solution)/shard_map/while/body/eval_jaxpr/ppermute | solution.py:12
  397.0 20.9 %collective-permute-start = (bf16[352,1024]{1,0:T(8,128)(2,1)S(1)}, bf16[352,1024]{1,0:T(8,128)(2,1)}, u32[]{:S(2)}, u32[]{:S(2)}) collective-permute-start(bf16[352,1024]{1,0:T(8,128)(2,1)S(1)} %copy.16), channel_id=1, source_target_pairs={{0,8},{8,16},{16,24},{24,32},{32,40},{40,48},{48,56},{56,64},{64,7... | collective-permute-start | bytes 2162696 | tf_op jit(solution)/shard_map/while/body/eval_jaxpr/ppermute | solution.py:12
  423.5 13.1 %collective-permute-start.1 = (bf16[352,1024]{1,0:T(8,128)(2,1)}, bf16[352,1024]{1,0:T(8,128)(2,1)}, u32[]{:S(2)}, u32[]{:S(2)}) collective-permute-start(bf16[352,1024]{1,0:T(8,128)(2,1)} %fusion.49), channel_id=1, source_target_pairs={{0,8},{8,16},{16,24},{24,32},{32,40},{40,48},{48,56},{56,64},{64,7... | collective-permute-start | bytes 2162696 | tf_op jit(solution)/shard_map/while/body/eval_jaxpr/ppermute | solution.py:12
  423.5 20.9 %collective-permute-start = (bf16[352,1024]{1,0:T(8,128)(2,1)S(1)}, bf16[352,1024]{1,0:T(8,128)(2,1)}, u32[]{:S(2)}, u32[]{:S(2)}) collective-permute-start(bf16[352,1024]{1,0:T(8,128)(2,1)S(1)} %copy.16), channel_id=1, source_target_pairs={{0,8},{8,16},{16,24},{24,32},{32,40},{40,48},{48,56},{56,64},{64,7... | collective-permute-start | bytes 2162696 | tf_op jit(solution)/shard_map/while/body/eval_jaxpr/ppermute | solution.py:12
  450.0 13.1 %collective-permute-start.1 = (bf16[352,1024]{1,0:T(8,128)(2,1)}, bf16[352,1024]{1,0:T(8,128)(2,1)}, u32[]{:S(2)}, u32[]{:S(2)}) collective-permute-start(bf16[352,1024]{1,0:T(8,128)(2,1)} %fusion.49), channel_id=1, source_target_pairs={{0,8},{8,16},{16,24},{24,32},{32,40},{40,48},{48,56},{56,64},{64,7... | collective-permute-start | bytes 2162696 | tf_op jit(solution)/shard_map/while/body/eval_jaxpr/ppermute | solution.py:12
  450.0 20.9 %collective-permute-start = (bf16[352,1024]{1,0:T(8,128)(2,1)S(1)}, bf16[352,1024]{1,0:T(8,128)(2,1)}, u32[]{:S(2)}, u32[]{:S(2)}) collective-permute-start(bf16[352,1024]{1,0:T(8,128)(2,1)S(1)} %copy.16), channel_id=1, source_target_pairs={{0,8},{8,16},{16,24},{24,32},{32,40},{40,48},{48,56},{56,64},{64,7... | collective-permute-start | bytes 2162696 | tf_op jit(solution)/shard_map/while/body/eval_jaxpr/ppermute | solution.py:12
  476.6 13.1 %collective-permute-start.1 = (bf16[352,1024]{1,0:T(8,128)(2,1)}, bf16[352,1024]{1,0:T(8,128)(2,1)}, u32[]{:S(2)}, u32[]{:S(2)}) collective-permute-start(bf16[352,1024]{1,0:T(8,128)(2,1)} %fusion.49), channel_id=1, source_target_pairs={{0,8},{8,16},{16,24},{24,32},{32,40},{40,48},{48,56},{56,64},{64,7... | collective-permute-start | bytes 2162696 | tf_op jit(solution)/shard_map/while/body/eval_jaxpr/ppermute | solution.py:12
  476.6 20.9 %collective-permute-start = (bf16[352,1024]{1,0:T(8,128)(2,1)S(1)}, bf16[352,1024]{1,0:T(8,128)(2,1)}, u32[]{:S(2)}, u32[]{:S(2)}) collective-permute-start(bf16[352,1024]{1,0:T(8,128)(2,1)S(1)} %copy.16), channel_id=1, source_target_pairs={{0,8},{8,16},{16,24},{24,32},{32,40},{40,48},{48,56},{56,64},{64,7... | collective-permute-start | bytes 2162696 | tf_op jit(solution)/shard_map/while/body/eval_jaxpr/ppermute | solution.py:12
  503.1 13.1 %collective-permute-start.1 = (bf16[352,1024]{1,0:T(8,128)(2,1)}, bf16[352,1024]{1,0:T(8,128)(2,1)}, u32[]{:S(2)}, u32[]{:S(2)}) collective-permute-start(bf16[352,1024]{1,0:T(8,128)(2,1)} %fusion.49), channel_id=1, source_target_pairs={{0,8},{8,16},{16,24},{24,32},{32,40},{40,48},{48,56},{56,64},{64,7... | collective-permute-start | bytes 2162696 | tf_op jit(solution)/shard_map/while/body/eval_jaxpr/ppermute | solution.py:12
  503.1 20.9 %collective-permute-start = (bf16[352,1024]{1,0:T(8,128)(2,1)S(1)}, bf16[352,1024]{1,0:T(8,128)(2,1)}, u32[]{:S(2)}, u32[]{:S(2)}) collective-permute-start(bf16[352,1024]{1,0:T(8,128)(2,1)S(1)} %copy.16), channel_id=1, source_target_pairs={{0,8},{8,16},{16,24},{24,32},{32,40},{40,48},{48,56},{56,64},{64,7... | collective-permute-start | bytes 2162696 | tf_op jit(solution)/shard_map/while/body/eval_jaxpr/ppermute | solution.py:12
  529.7 13.1 %collective-permute-start.1 = (bf16[352,1024]{1,0:T(8,128)(2,1)}, bf16[352,1024]{1,0:T(8,128)(2,1)}, u32[]{:S(2)}, u32[]{:S(2)}) collective-permute-start(bf16[352,1024]{1,0:T(8,128)(2,1)} %fusion.49), channel_id=1, source_target_pairs={{0,8},{8,16},{16,24},{24,32},{32,40},{40,48},{48,56},{56,64},{64,7... | collective-permute-start | bytes 2162696 | tf_op jit(solution)/shard_map/while/body/eval_jaxpr/ppermute | solution.py:12
  529.7 20.9 %collective-permute-start = (bf16[352,1024]{1,0:T(8,128)(2,1)S(1)}, bf16[352,1024]{1,0:T(8,128)(2,1)}, u32[]{:S(2)}, u32[]{:S(2)}) collective-permute-start(bf16[352,1024]{1,0:T(8,128)(2,1)S(1)} %copy.16), channel_id=1, source_target_pairs={{0,8},{8,16},{16,24},{24,32},{32,40},{40,48},{48,56},{56,64},{64,7... | collective-permute-start | bytes 2162696 | tf_op jit(solution)/shard_map/while/body/eval_jaxpr/ppermute | solution.py:12
  550.5 1.8 copy-start.3
  552.3 1.6 copy-start.7
  555.9 1.2 copy-start.1
  555.9 1.6 copy-start.6
  557.5 1.6 copy-start.4
Sparse Core Ops, SparseCore 0:
  10.2 57.0 all-gather.4
  69.5 52.3 all-gather.2
  557.3 66.8 reduce-scatter.3
where the time goes:
time: 636 us; the launch traced here: 632 us
  waiting for transfers between devices  448 us (70%)
  matrix products  93.8 us (15%)
  other arithmetic  50.7 us (8%)
  local copies, waits for them, and re-layouts  23.7 us (4%)
  between operations  13.9 us (2%)
    ppermute x32, waiting for transfers between devices, passed_along(): return lax.ppermute(value, axis, pairs)  276 us
    unnamed x4, waiting for transfers between devices  64 us
    all_gather x1, waiting for transfers between devices, body(): lax.all_gather(sentence_projector_matrix, 'tensor', axis=1, tiled=True)  56.4 us
    all_gather x1, waiting for transfers between devices, body(): lax.all_gather(picture_projector_matrix, 'tensor', axis=1, tiled=True)  52.2 us
    dot_general x16, matrix products, step(): jnp.einsum('mc,me->ce', pair_factor, block_z, preferred_element_type=jnp....  36.3 us
    dot_general x16, matrix products, image_tile(): jnp.einsum('me,ce->mc', block_z, cap_z, preferred_element_type=jnp.float32)  28.3 us
    convert_element_type x16, other arithmetic, step(): passed_along(carried.astype(jnp.bfloat16), 'dp', 1).astype(carried.dtype)  20.1 us
    dot_general x16, matrix products, step(): jnp.dot(pair_factor, cap_z, preferred_element_type=jnp.float32)  19.8 us
  transfers between devices with their start and end apart: 35, of which 35 were waited for; matrix products, arithmetic and copies ran while one was open for 10% of the time, Pallas kernels for 0%

commit v1 on v0

--- a/solution.py
+++ b/solution.py
@@ -61,7 +61,12 @@
     score_offset_term,
 ):
     full_img, full_cap = (
-        lax.all_gather(picture_projector_matrix, "tensor", axis=1, tiled=True),
+        jnp.concatenate(
+            lax.all_to_all(
+                jnp.stack([picture_projector_matrix] * lax.axis_size("tensor")), "tensor", 0, 0
+            ),
+            axis=1,
+        ),
         lax.all_gather(sentence_projector_matrix, "tensor", axis=1, tiled=True),
     )
     img_unit, img_scale = embed(picture_encoder_result, full_img)

time: 636 us -> 576 us (0.906)
  waiting for transfers between devices: 448 us -> 397 us
  other arithmetic: 50.7 us -> 26.7 us
  starting transfers between devices: 1.78 us -> 9.9 us
    all_gather x1 -> x0, waiting for transfers between devices: 52.2 us -> none  [body(): lax.all_gather(picture_projector_matrix, 'tensor', axis=1, tiled=True)]
    all_to_all x0 -> x1, waiting for transfers between devices: none -> 28.6 us  [body(): lax.all_to_all(jnp.stack([picture_projector_matrix] * lax.axis_size('tens...]
    all_gather x1, waiting for transfers between devices: 56.4 us -> 30 us  [body(): lax.all_gather(sentence_projector_matrix, 'tensor', axis=1, tiled=True)]
    add x16, other arithmetic: 12.4 us -> 1.24 us  [scaling_factor(): other_begin_list + sentence_tally_later]
    div x16, other arithmetic: 12.3 us -> 1.24 us  [scaling_factor(): 1.0 / sentence_tally_later.astype(jnp.float32)]
    all_to_all x0 -> x1, starting transfers between devices: none -> 8.16 us  [body(): lax.all_to_all(jnp.stack([picture_projector_matrix] * lax.axis_size('tens...]
    unnamed x4 -> x3, waiting for transfers between devices: 64 us -> 63.3 us
  transfers between devices with their start and end apart: 35 -> 35, of which waited for: 35 -> 35; matrix products, arithmetic and copies ran while one was open for 10% -> 12% of each run, Pallas kernels for 0% -> 0%
where the time goes in v1:
time: 576 us; the launch traced here: 573 us
  waiting for transfers between devices  397 us (69%)
  matrix products  97 us (17%)
  local copies, waits for them, and re-layouts  27.1 us (5%)
  other arithmetic  26.7 us (5%)
  between operations  14.2 us (2%)
  starting transfers between devices  9.9 us (2%)
    ppermute x32, waiting for transfers between devices, passed_along(): return lax.ppermute(value, axis, pairs)  276 us
    unnamed x3, waiting for transfers between devices  63.3 us
    dot_general x16, matrix products, step(): jnp.einsum('mc,me->ce', pair_factor, block_z, preferred_element_type=jnp....  36.2 us
    all_gather x1, waiting for transfers between devices, body(): lax.all_gather(sentence_projector_matrix, 'tensor', axis=1, tiled=True)  30 us
    all_to_all x1, waiting for transfers between devices, body(): lax.all_to_all(jnp.stack([picture_projector_matrix] * lax.axis_size('tens...  28.6 us
    dot_general x16, matrix products, image_tile(): jnp.einsum('me,ce->mc', block_z, cap_z, preferred_element_type=jnp.float32)  28.4 us
    convert_element_type x16, other arithmetic, step(): passed_along(carried.astype(jnp.bfloat16), 'dp', 1).astype(carried.dtype)  20.1 us
    dot_general x16, matrix products, step(): jnp.dot(pair_factor, cap_z, preferred_element_type=jnp.float32)  19.8 us
  transfers between devices with their start and end apart: 35, of which 35 were waited for; matrix products, arithmetic and copies ran while one was open for 12% of the time, Pallas kernels for 0%

profile of v1, /device:TPU:0, one launch (start us, length us, event | category | flops | bytes accessed | tf_op | source)
XLA Modules:
  0.0 572.7 jit_solution(10570389925784544157)
XLA Ops:
  10.6 8.2 %all-to-all-start = ((bf16[8,1024,128]{1,2,0:T(8,128)(2,1)}), bf16[8,1024,128]{1,2,0:T(8,128)(2,1)}, u32[]{:S(2)}, u32[]{:S(2)}) async-start(bf16[8,1024,128]{1,2,0:T(8,128)(2,1)} %stack.2), calls=%async_computation | async-start | bytes 4194304 | tf_op jit(solution)/shard_map/all_to_all | solution.py:65
  19.5 28.6 %all-to-all-done = bf16[8,1024,128]{1,2,0:T(8,128)(2,1)} async-done(((bf16[8,1024,128]{1,2,0:T(8,128)(2,1)}), bf16[8,1024,128]{1,2,0:T(8,128)(2,1)}, u32[]{:S(2)}, u32[]{:S(2)}) %all-to-all-start) | async-done | bytes 2097184 | tf_op jit(solution)/shard_map/all_to_all | solution.py:65
  48.0 2.7 multiply_reduce_fusion.1
  52.9 30.0 %all-gather.2.cloned.1.call-done = bf16[1024,1024]{1,0:T(8,128)(2,1)} async-done(((bf16[1024,128]{1,0:T(8,128)(2,1)}), bf16[1024,1024]{1,0:T(8,128)(2,1)}) %all-gather.2.cloned.1.call-update) | async-done | bytes 2097168 | tf_op jit(solution)/shard_map/all_gather | solution.py:70
  82.9 2.2 multiply_reduce_fusion.3
  86.1 402.7 %while.20 = (s32[]{:T(128)}, bf16[352,1024]{1,0:T(8,128)(2,1)}, f32[352,1024]{1,0:T(8,128)S(1)}, f32[176,1024]{1,0:T(8,128)}, f32[]{:T(128)}, /*index=5*/s32[]{:...) while((s32[]{:T(128)}, bf16[352,1024]{1,0:T(8,128)(2,1)}, ...), condition=%wide.region_5.6_spmd.clone, body=%wide.region_4.5_spmd.clone.sunk | while | flops 383427808 | bytes 15525043 | solution.py:127
  87.4 1.8 fusion.48
  93.3 10.3 %collective-permute-done.1 = bf16[352,1024]{1,0:T(8,128)(2,1)} collective-permute-done((bf16[352,1024]{1,0:T(8,128)(2,1)}, bf16[352,1024]{1,0:T(8,128)(2,1)}, u32[]{:S(2)}, u32[]{:S(2)}) %collective-permute-start.1) | collective-permute-done | bytes 720928 | tf_op jit(solution)/shard_map/while/body/eval_jaxpr/ppermute | solution.py:12
  104.9 6.5 %collective-permute-done = bf16[352,1024]{1,0:T(8,128)(2,1)} collective-permute-done((bf16[352,1024]{1,0:T(8,128)(2,1)S(1)}, bf16[352,1024]{1,0:T(8,128)(2,1)}, u32[]{:S(2)}, u32[]{:S(2)}) %collective-permute-start) | collective-permute-done | bytes 720928 | tf_op jit(solution)/shard_map/while/body/eval_jaxpr/ppermute | solution.py:12
  112.6 1.8 fusion.48
  115.6 2.3 convolution_add_fusion.5
  118.0 10.8 %collective-permute-done.1 = bf16[352,1024]{1,0:T(8,128)(2,1)} collective-permute-done((bf16[352,1024]{1,0:T(8,128)(2,1)}, bf16[352,1024]{1,0:T(8,128)(2,1)}, u32[]{:S(2)}, u32[]{:S(2)}) %collective-permute-start.1) | collective-permute-done | bytes 720928 | tf_op jit(solution)/shard_map/while/body/eval_jaxpr/ppermute | solution.py:12
  130.0 6.5 %collective-permute-done = bf16[352,1024]{1,0:T(8,128)(2,1)} collective-permute-done((bf16[352,1024]{1,0:T(8,128)(2,1)S(1)}, bf16[352,1024]{1,0:T(8,128)(2,1)}, u32[]{:S(2)}, u32[]{:S(2)}) %collective-permute-start) | collective-permute-done | bytes 720928 | tf_op jit(solution)/shard_map/while/body/eval_jaxpr/ppermute | solution.py:12
  137.7 1.8 fusion.48
  140.8 2.3 convolution_add_fusion.5
  143.1 10.8 %collective-permute-done.1 = bf16[352,1024]{1,0:T(8,128)(2,1)} collective-permute-done((bf16[352,1024]{1,0:T(8,128)(2,1)}, bf16[352,1024]{1,0:T(8,128)(2,1)}, u32[]{:S(2)}, u32[]{:S(2)}) %collective-permute-start.1) | collective-permute-done | bytes 720928 | tf_op jit(solution)/shard_map/while/body/eval_jaxpr/ppermute | solution.py:12
  155.2 6.5 %collective-permute-done = bf16[352,1024]{1,0:T(8,128)(2,1)} collective-permute-done((bf16[352,1024]{1,0:T(8,128)(2,1)S(1)}, bf16[352,1024]{1,0:T(8,128)(2,1)}, u32[]{:S(2)}, u32[]{:S(2)}) %collective-permute-start) | collective-permute-done | bytes 720928 | tf_op jit(solution)/shard_map/while/body/eval_jaxpr/ppermute | solution.py:12
  162.9 1.8 fusion.48
  165.9 2.3 convolution_add_fusion.5
  168.3 10.8 %collective-permute-done.1 = bf16[352,1024]{1,0:T(8,128)(2,1)} collective-permute-done((bf16[352,1024]{1,0:T(8,128)(2,1)}, bf16[352,1024]{1,0:T(8,128)(2,1)}, u32[]{:S(2)}, u32[]{:S(2)}) %collective-permute-start.1) | collective-permute-done | bytes 720928 | tf_op jit(solution)/shard_map/while/body/eval_jaxpr/ppermute | solution.py:12
  180.3 6.5 %collective-permute-done = bf16[352,1024]{1,0:T(8,128)(2,1)} collective-permute-done((bf16[352,1024]{1,0:T(8,128)(2,1)S(1)}, bf16[352,1024]{1,0:T(8,128)(2,1)}, u32[]{:S(2)}, u32[]{:S(2)}) %collective-permute-start) | collective-permute-done | bytes 720928 | tf_op jit(solution)/shard_map/while/body/eval_jaxpr/ppermute | solution.py:12
  191.1 2.3 convolution_add_fusion.5
  193.4 10.8 %collective-permute-done.1 = bf16[352,1024]{1,0:T(8,128)(2,1)} collective-permute-done((bf16[352,1024]{1,0:T(8,128)(2,1)}, bf16[352,1024]{1,0:T(8,128)(2,1)}, u32[]{:S(2)}, u32[]{:S(2)}) %collective-permute-start.1) | collective-permute-done | bytes 720928 | tf_op jit(solution)/shard_map/while/body/eval_jaxpr/ppermute | solution.py:12
  205.5 6.5 %collective-permute-done = bf16[352,1024]{1,0:T(8,128)(2,1)} collective-permute-done((bf16[352,1024]{1,0:T(8,128)(2,1)S(1)}, bf16[352,1024]{1,0:T(8,128)(2,1)}, u32[]{:S(2)}, u32[]{:S(2)}) %collective-permute-start) | collective-permute-done | bytes 720928 | tf_op jit(solution)/shard_map/while/body/eval_jaxpr/ppermute | solution.py:12
  213.2 1.8 fusion.48
  216.3 2.3 convolution_add_fusion.5
  218.6 10.8 %collective-permute-done.1 = bf16[352,1024]{1,0:T(8,128)(2,1)} collective-permute-done((bf16[352,1024]{1,0:T(8,128)(2,1)}, bf16[352,1024]{1,0:T(8,128)(2,1)}, u32[]{:S(2)}, u32[]{:S(2)}) %collective-permute-start.1) | collective-permute-done | bytes 720928 | tf_op jit(solution)/shard_map/while/body/eval_jaxpr/ppermute | solution.py:12
  230.7 6.5 %collective-permute-done = bf16[352,1024]{1,0:T(8,128)(2,1)} collective-permute-done((bf16[352,1024]{1,0:T(8,128)(2,1)S(1)}, bf16[352,1024]{1,0:T(8,128)(2,1)}, u32[]{:S(2)}, u32[]{:S(2)}) %collective-permute-start) | collective-permute-done | bytes 720928 | tf_op jit(solution)/shard_map/while/body/eval_jaxpr/ppermute | solution.py:12
  241.4 2.3 convolution_add_fusion.5
  243.8 10.8 %collective-permute-done.1 = bf16[352,1024]{1,0:T(8,128)(2,1)} collective-permute-done((bf16[352,1024]{1,0:T(8,128)(2,1)}, bf16[352,1024]{1,0:T(8,128)(2,1)}, u32[]{:S(2)}, u32[]{:S(2)}) %collective-permute-start.1) | collective-permute-done | bytes 720928 | tf_op jit(solution)/shard_map/while/body/eval_jaxpr/ppermute | solution.py:12
  255.8 6.5 %collective-permute-done = bf16[352,1024]{1,0:T(8,128)(2,1)} collective-permute-done((bf16[352,1024]{1,0:T(8,128)(2,1)S(1)}, bf16[352,1024]{1,0:T(8,128)(2,1)}, u32[]{:S(2)}, u32[]{:S(2)}) %collective-permute-start) | collective-permute-done | bytes 720928 | tf_op jit(solution)/shard_map/while/body/eval_jaxpr/ppermute | solution.py:12
  263.6 1.8 fusion.48
  266.6 2.3 convolution_add_fusion.5
  268.9 10.8 %collective-permute-done.1 = bf16[352,1024]{1,0:T(8,128)(2,1)} collective-permute-done((bf16[352,1024]{1,0:T(8,128)(2,1)}, bf16[352,1024]{1,0:T(8,128)(2,1)}, u32[]{:S(2)}, u32[]{:S(2)}) %collective-permute-start.1) | collective-permute-done | bytes 720928 | tf_op jit(solution)/shard_map/while/body/eval_jaxpr/ppermute | solution.py:12
  281.0 6.5 %collective-permute-done = bf16[352,1024]{1,0:T(8,128)(2,1)} collective-permute-done((bf16[352,1024]{1,0:T(8,128)(2,1)S(1)}, bf16[352,1024]{1,0:T(8,128)(2,1)}, u32[]{:S(2)}, u32[]{:S(2)}) %collective-permute-start) | collective-permute-done | bytes 720928 | tf_op jit(solution)/shard_map/while/body/eval_jaxpr/ppermute | solution.py:12
  291.8 2.3 convolution_add_fusion.5
  294.1 10.8 %collective-permute-done.1 = bf16[352,1024]{1,0:T(8,128)(2,1)} collective-permute-done((bf16[352,1024]{1,0:T(8,128)(2,1)}, bf16[352,1024]{1,0:T(8,128)(2,1)}, u32[]{:S(2)}, u32[]{:S(2)}) %collective-permute-start.1) | collective-permute-done | bytes 720928 | tf_op jit(solution)/shard_map/while/body/eval_jaxpr/ppermute | solution.py:12
  306.2 6.5 %collective-permute-done = bf16[352,1024]{1,0:T(8,128)(2,1)} collective-permute-done((bf16[352,1024]{1,0:T(8,128)(2,1)S(1)}, bf16[352,1024]{1,0:T(8,128)(2,1)}, u32[]{:S(2)}, u32[]{:S(2)}) %collective-permute-start) | collective-permute-done | bytes 720928 | tf_op jit(solution)/shard_map/while/body/eval_jaxpr/ppermute | solution.py:12
  316.9 2.3 convolution_add_fusion.5
  319.3 10.8 %collective-permute-done.1 = bf16[352,1024]{1,0:T(8,128)(2,1)} collective-permute-done((bf16[352,1024]{1,0:T(8,128)(2,1)}, bf16[352,1024]{1,0:T(8,128)(2,1)}, u32[]{:S(2)}, u32[]{:S(2)}) %collective-permute-start.1) | collective-permute-done | bytes 720928 | tf_op jit(solution)/shard_map/while/body/eval_jaxpr/ppermute | solution.py:12
  331.3 6.5 %collective-permute-done = bf16[352,1024]{1,0:T(8,128)(2,1)} collective-permute-done((bf16[352,1024]{1,0:T(8,128)(2,1)S(1)}, bf16[352,1024]{1,0:T(8,128)(2,1)}, u32[]{:S(2)}, u32[]{:S(2)}) %collective-permute-start) | collective-permute-done | bytes 720928 | tf_op jit(solution)/shard_map/while/body/eval_jaxpr/ppermute | solution.py:12
  342.1 2.3 convolution_add_fusion.5
  344.4 10.8 %collective-permute-done.1 = bf16[352,1024]{1,0:T(8,128)(2,1)} collective-permute-done((bf16[352,1024]{1,0:T(8,128)(2,1)}, bf16[352,1024]{1,0:T(8,128)(2,1)}, u32[]{:S(2)}, u32[]{:S(2)}) %collective-permute-start.1) | collective-permute-done | bytes 720928 | tf_op jit(solution)/shard_map/while/body/eval_jaxpr/ppermute | solution.py:12
  356.5 6.5 %collective-permute-done = bf16[352,1024]{1,0:T(8,128)(2,1)} collective-permute-done((bf16[352,1024]{1,0:T(8,128)(2,1)S(1)}, bf16[352,1024]{1,0:T(8,128)(2,1)}, u32[]{:S(2)}, u32[]{:S(2)}) %collective-permute-start) | collective-permute-done | bytes 720928 | tf_op jit(solution)/shard_map/while/body/eval_jaxpr/ppermute | solution.py:12
  364.2 1.8 fusion.48
  367.2 2.3 convolution_add_fusion.5
  369.6 10.8 %collective-permute-done.1 = bf16[352,1024]{1,0:T(8,128)(2,1)} collective-permute-done((bf16[352,1024]{1,0:T(8,128)(2,1)}, bf16[352,1024]{1,0:T(8,128)(2,1)}, u32[]{:S(2)}, u32[]{:S(2)}) %collective-permute-start.1) | collective-permute-done | bytes 720928 | tf_op jit(solution)/shard_map/while/body/eval_jaxpr/ppermute | solution.py:12
  381.6 6.5 %collective-permute-done = bf16[352,1024]{1,0:T(8,128)(2,1)} collective-permute-done((bf16[352,1024]{1,0:T(8,128)(2,1)S(1)}, bf16[352,1024]{1,0:T(8,128)(2,1)}, u32[]{:S(2)}, u32[]{:S(2)}) %collective-permute-start) | collective-permute-done | bytes 720928 | tf_op jit(solution)/shard_map/while/body/eval_jaxpr/ppermute | solution.py:12
  392.4 2.3 convolution_add_fusion.5
  394.7 10.8 %collective-permute-done.1 = bf16[352,1024]{1,0:T(8,128)(2,1)} collective-permute-done((bf16[352,1024]{1,0:T(8,128)(2,1)}, bf16[352,1024]{1,0:T(8,128)(2,1)}, u32[]{:S(2)}, u32[]{:S(2)}) %collective-permute-start.1) | collective-permute-done | bytes 720928 | tf_op jit(solution)/shard_map/while/body/eval_jaxpr/ppermute | solution.py:12
  406.8 6.5 %collective-permute-done = bf16[352,1024]{1,0:T(8,128)(2,1)} collective-permute-done((bf16[352,1024]{1,0:T(8,128)(2,1)S(1)}, bf16[352,1024]{1,0:T(8,128)(2,1)}, u32[]{:S(2)}, u32[]{:S(2)}) %collective-permute-start) | collective-permute-done | bytes 720928 | tf_op jit(solution)/shard_map/while/body/eval_jaxpr/ppermute | solution.py:12
  417.6 2.3 convolution_add_fusion.5
  419.9 10.8 %collective-permute-done.1 = bf16[352,1024]{1,0:T(8,128)(2,1)} collective-permute-done((bf16[352,1024]{1,0:T(8,128)(2,1)}, bf16[352,1024]{1,0:T(8,128)(2,1)}, u32[]{:S(2)}, u32[]{:S(2)}) %collective-permute-start.1) | collective-permute-done | bytes 720928 | tf_op jit(solution)/shard_map/while/body/eval_jaxpr/ppermute | solution.py:12
  432.0 6.5 %collective-permute-done = bf16[352,1024]{1,0:T(8,128)(2,1)} collective-permute-done((bf16[352,1024]{1,0:T(8,128)(2,1)S(1)}, bf16[352,1024]{1,0:T(8,128)(2,1)}, u32[]{:S(2)}, u32[]{:S(2)}) %collective-permute-start) | collective-permute-done | bytes 720928 | tf_op jit(solution)/shard_map/while/body/eval_jaxpr/ppermute | solution.py:12
  442.7 2.3 convolution_add_fusion.5
  445.1 10.8 %collective-permute-done.1 = bf16[352,1024]{1,0:T(8,128)(2,1)} collective-permute-done((bf16[352,1024]{1,0:T(8,128)(2,1)}, bf16[352,1024]{1,0:T(8,128)(2,1)}, u32[]{:S(2)}, u32[]{:S(2)}) %collective-permute-start.1) | collective-permute-done | bytes 720928 | tf_op jit(solution)/shard_map/while/body/eval_jaxpr/ppermute | solution.py:12
  457.1 6.5 %collective-permute-done = bf16[352,1024]{1,0:T(8,128)(2,1)} collective-permute-done((bf16[352,1024]{1,0:T(8,128)(2,1)S(1)}, bf16[352,1024]{1,0:T(8,128)(2,1)}, u32[]{:S(2)}, u32[]{:S(2)}) %collective-permute-start) | collective-permute-done | bytes 720928 | tf_op jit(solution)/shard_map/while/body/eval_jaxpr/ppermute | solution.py:12
  464.9 1.8 fusion.48
  467.9 2.3 convolution_add_fusion.5
  470.2 10.8 %collective-permute-done.1 = bf16[352,1024]{1,0:T(8,128)(2,1)} collective-permute-done((bf16[352,1024]{1,0:T(8,128)(2,1)}, bf16[352,1024]{1,0:T(8,128)(2,1)}, u32[]{:S(2)}, u32[]{:S(2)}) %collective-permute-start.1) | collective-permute-done | bytes 720928 | tf_op jit(solution)/shard_map/while/body/eval_jaxpr/ppermute | solution.py:12
  482.3 6.5 %collective-permute-done = bf16[352,1024]{1,0:T(8,128)(2,1)} collective-permute-done((bf16[352,1024]{1,0:T(8,128)(2,1)S(1)}, bf16[352,1024]{1,0:T(8,128)(2,1)}, u32[]{:S(2)}, u32[]{:S(2)}) %collective-permute-start) | collective-permute-done | bytes 720928 | tf_op jit(solution)/shard_map/while/body/eval_jaxpr/ppermute | solution.py:12
  490.9 2.5 fusion.16
  493.4 2.6 fusion.12
  501.7 62.6 %reduce-scatter.4.cloned.1.call-done = bf16[128,352]{1,0:T(8,128)(2,1)} async-done(((bf16[1024,352]{1,0:T(8,128)(2,1)}), bf16[128,352]{1,0:T(8,128)(2,1)}) %reduce-scatter.4.cloned.1.call-update) | async-done | bytes 90128
  (180 shorter events, 94.0 us)
Async XLA Ops:
  7.2 40.9 %copy-start = (bf16[352,1024]{1,0:T(8,128)(2,1)S(1)}, bf16[352,1024]{1,0:T(8,128)(2,1)}, u32[]{:S(2)}) copy-start(bf16[352,1024]{1,0:T(8,128)(2,1)} %param.9) | copy-start | bytes 2162692
  7.2 75.7 %all-gather.2.cloned.1.call-start = ((), (), s32[]{:S(2)}) async-start(), calls=%async_computation.2 | async-start | bytes 2359296 | tf_op jit(solution)/shard_map/all_gather | solution.py:70
  10.6 8.2 %copy-start.8 = (s32[5632]{0:T(1024)S(1)}, s32[5632]{0:T(1024)}, u32[]{:S(2)}) copy-start(s32[5632]{0:T(1024)} %param.13) | copy-start | bytes 67588
  10.6 37.4 %all-to-all-start = ((bf16[8,1024,128]{1,2,0:T(8,128)(2,1)}), bf16[8,1024,128]{1,2,0:T(8,128)(2,1)}, u32[]{:S(2)}, u32[]{:S(2)}) async-start(bf16[8,1024,128]{1,2,0:T(8,128)(2,1)} %stack.2), calls=%async_computation | async-start | bytes 4194304 | tf_op jit(solution)/shard_map/all_to_all | solution.py:65
  18.8 545.5 %reduce-scatter.4.cloned.1.call-start = ((), (), s32[]{:S(2)}) async-start(), calls=%async_computation.3 | async-start | bytes 884736
  50.7 1.1 copy-start.2
  50.7 32.2 %copy-start.7 = (bf16[176,1024]{1,0:T(8,128)(2,1)S(1)}, bf16[176,1024]{1,0:T(8,128)(2,1)}, u32[]{:S(2)}) copy-start(bf16[176,1024]{1,0:T(8,128)(2,1)} %param.10) | copy-start | bytes 1081348
  85.1 0.9 copy-start.5
  90.4 13.1 %collective-permute-start.1 = (bf16[352,1024]{1,0:T(8,128)(2,1)}, bf16[352,1024]{1,0:T(8,128)(2,1)}, u32[]{:S(2)}, u32[]{:S(2)}) collective-permute-start(bf16[352,1024]{1,0:T(8,128)(2,1)} %fusion.49), channel_id=1, source_target_pairs={{0,8},{8,16},{16,24},{24,32},{32,40},{40,48},{48,56},{56,64},{64,7... | collective-permute-start | bytes 2162696 | tf_op jit(solution)/shard_map/while/body/eval_jaxpr/ppermute | solution.py:12
  90.5 20.9 %collective-permute-start = (bf16[352,1024]{1,0:T(8,128)(2,1)S(1)}, bf16[352,1024]{1,0:T(8,128)(2,1)}, u32[]{:S(2)}, u32[]{:S(2)}) collective-permute-start(bf16[352,1024]{1,0:T(8,128)(2,1)S(1)} %copy.18), channel_id=1, source_target_pairs={{0,8},{8,16},{16,24},{24,32},{32,40},{40,48},{48,56},{56,64},{64,7... | collective-permute-start | bytes 2162696 | tf_op jit(solution)/shard_map/while/body/eval_jaxpr/ppermute | solution.py:12
  115.6 13.1 %collective-permute-start.1 = (bf16[352,1024]{1,0:T(8,128)(2,1)}, bf16[352,1024]{1,0:T(8,128)(2,1)}, u32[]{:S(2)}, u32[]{:S(2)}) collective-permute-start(bf16[352,1024]{1,0:T(8,128)(2,1)} %fusion.49), channel_id=1, source_target_pairs={{0,8},{8,16},{16,24},{24,32},{32,40},{40,48},{48,56},{56,64},{64,7... | collective-permute-start | bytes 2162696 | tf_op jit(solution)/shard_map/while/body/eval_jaxpr/ppermute | solution.py:12
  115.6 20.9 %collective-permute-start = (bf16[352,1024]{1,0:T(8,128)(2,1)S(1)}, bf16[352,1024]{1,0:T(8,128)(2,1)}, u32[]{:S(2)}, u32[]{:S(2)}) collective-permute-start(bf16[352,1024]{1,0:T(8,128)(2,1)S(1)} %copy.18), channel_id=1, source_target_pairs={{0,8},{8,16},{16,24},{24,32},{32,40},{40,48},{48,56},{56,64},{64,7... | collective-permute-start | bytes 2162696 | tf_op jit(solution)/shard_map/while/body/eval_jaxpr/ppermute | solution.py:12
  140.8 13.1 %collective-permute-start.1 = (bf16[352,1024]{1,0:T(8,128)(2,1)}, bf16[352,1024]{1,0:T(8,128)(2,1)}, u32[]{:S(2)}, u32[]{:S(2)}) collective-permute-start(bf16[352,1024]{1,0:T(8,128)(2,1)} %fusion.49), channel_id=1, source_target_pairs={{0,8},{8,16},{16,24},{24,32},{32,40},{40,48},{48,56},{56,64},{64,7... | collective-permute-start | bytes 2162696 | tf_op jit(solution)/shard_map/while/body/eval_jaxpr/ppermute | solution.py:12
  140.8 20.9 %collective-permute-start = (bf16[352,1024]{1,0:T(8,128)(2,1)S(1)}, bf16[352,1024]{1,0:T(8,128)(2,1)}, u32[]{:S(2)}, u32[]{:S(2)}) collective-permute-start(bf16[352,1024]{1,0:T(8,128)(2,1)S(1)} %copy.18), channel_id=1, source_target_pairs={{0,8},{8,16},{16,24},{24,32},{32,40},{40,48},{48,56},{56,64},{64,7... | collective-permute-start | bytes 2162696 | tf_op jit(solution)/shard_map/while/body/eval_jaxpr/ppermute | solution.py:12
  165.9 13.1 %collective-permute-start.1 = (bf16[352,1024]{1,0:T(8,128)(2,1)}, bf16[352,1024]{1,0:T(8,128)(2,1)}, u32[]{:S(2)}, u32[]{:S(2)}) collective-permute-start(bf16[352,1024]{1,0:T(8,128)(2,1)} %fusion.49), channel_id=1, source_target_pairs={{0,8},{8,16},{16,24},{24,32},{32,40},{40,48},{48,56},{56,64},{64,7... | collective-permute-start | bytes 2162696 | tf_op jit(solution)/shard_map/while/body/eval_jaxpr/ppermute | solution.py:12
  165.9 20.9 %collective-permute-start = (bf16[352,1024]{1,0:T(8,128)(2,1)S(1)}, bf16[352,1024]{1,0:T(8,128)(2,1)}, u32[]{:S(2)}, u32[]{:S(2)}) collective-permute-start(bf16[352,1024]{1,0:T(8,128)(2,1)S(1)} %copy.18), channel_id=1, source_target_pairs={{0,8},{8,16},{16,24},{24,32},{32,40},{40,48},{48,56},{56,64},{64,7... | collective-permute-start | bytes 2162696 | tf_op jit(solution)/shard_map/while/body/eval_jaxpr/ppermute | solution.py:12
  191.1 13.1 %collective-permute-start.1 = (bf16[352,1024]{1,0:T(8,128)(2,1)}, bf16[352,1024]{1,0:T(8,128)(2,1)}, u32[]{:S(2)}, u32[]{:S(2)}) collective-permute-start(bf16[352,1024]{1,0:T(8,128)(2,1)} %fusion.49), channel_id=1, source_target_pairs={{0,8},{8,16},{16,24},{24,32},{32,40},{40,48},{48,56},{56,64},{64,7... | collective-permute-start | bytes 2162696 | tf_op jit(solution)/shard_map/while/body/eval_jaxpr/ppermute | solution.py:12
  191.1 20.9 %collective-permute-start = (bf16[352,1024]{1,0:T(8,128)(2,1)S(1)}, bf16[352,1024]{1,0:T(8,128)(2,1)}, u32[]{:S(2)}, u32[]{:S(2)}) collective-permute-start(bf16[352,1024]{1,0:T(8,128)(2,1)S(1)} %copy.18), channel_id=1, source_target_pairs={{0,8},{8,16},{16,24},{24,32},{32,40},{40,48},{48,56},{56,64},{64,7... | collective-permute-start | bytes 2162696 | tf_op jit(solution)/shard_map/while/body/eval_jaxpr/ppermute | solution.py:12
  216.3 13.1 %collective-permute-start.1 = (bf16[352,1024]{1,0:T(8,128)(2,1)}, bf16[352,1024]{1,0:T(8,128)(2,1)}, u32[]{:S(2)}, u32[]{:S(2)}) collective-permute-start(bf16[352,1024]{1,0:T(8,128)(2,1)} %fusion.49), channel_id=1, source_target_pairs={{0,8},{8,16},{16,24},{24,32},{32,40},{40,48},{48,56},{56,64},{64,7... | collective-permute-start | bytes 2162696 | tf_op jit(solution)/shard_map/while/body/eval_jaxpr/ppermute | solution.py:12
  216.3 20.9 %collective-permute-start = (bf16[352,1024]{1,0:T(8,128)(2,1)S(1)}, bf16[352,1024]{1,0:T(8,128)(2,1)}, u32[]{:S(2)}, u32[]{:S(2)}) collective-permute-start(bf16[352,1024]{1,0:T(8,128)(2,1)S(1)} %copy.18), channel_id=1, source_target_pairs={{0,8},{8,16},{16,24},{24,32},{32,40},{40,48},{48,56},{56,64},{64,7... | collective-permute-start | bytes 2162696 | tf_op jit(solution)/shard_map/while/body/eval_jaxpr/ppermute | solution.py:12
  241.4 13.1 %collective-permute-start.1 = (bf16[352,1024]{1,0:T(8,128)(2,1)}, bf16[352,1024]{1,0:T(8,128)(2,1)}, u32[]{:S(2)}, u32[]{:S(2)}) collective-permute-start(bf16[352,1024]{1,0:T(8,128)(2,1)} %fusion.49), channel_id=1, source_target_pairs={{0,8},{8,16},{16,24},{24,32},{32,40},{40,48},{48,56},{56,64},{64,7... | collective-permute-start | bytes 2162696 | tf_op jit(solution)/shard_map/while/body/eval_jaxpr/ppermute | solution.py:12
  241.4 20.9 %collective-permute-start = (bf16[352,1024]{1,0:T(8,128)(2,1)S(1)}, bf16[352,1024]{1,0:T(8,128)(2,1)}, u32[]{:S(2)}, u32[]{:S(2)}) collective-permute-start(bf16[352,1024]{1,0:T(8,128)(2,1)S(1)} %copy.18), channel_id=1, source_target_pairs={{0,8},{8,16},{16,24},{24,32},{32,40},{40,48},{48,56},{56,64},{64,7... | collective-permute-start | bytes 2162696 | tf_op jit(solution)/shard_map/while/body/eval_jaxpr/ppermute | solution.py:12
  266.6 13.1 %collective-permute-start.1 = (bf16[352,1024]{1,0:T(8,128)(2,1)}, bf16[352,1024]{1,0:T(8,128)(2,1)}, u32[]{:S(2)}, u32[]{:S(2)}) collective-permute-start(bf16[352,1024]{1,0:T(8,128)(2,1)} %fusion.49), channel_id=1, source_target_pairs={{0,8},{8,16},{16,24},{24,32},{32,40},{40,48},{48,56},{56,64},{64,7... | collective-permute-start | bytes 2162696 | tf_op jit(solution)/shard_map/while/body/eval_jaxpr/ppermute | solution.py:12
  266.6 20.9 %collective-permute-start = (bf16[352,1024]{1,0:T(8,128)(2,1)S(1)}, bf16[352,1024]{1,0:T(8,128)(2,1)}, u32[]{:S(2)}, u32[]{:S(2)}) collective-permute-start(bf16[352,1024]{1,0:T(8,128)(2,1)S(1)} %copy.18), channel_id=1, source_target_pairs={{0,8},{8,16},{16,24},{24,32},{32,40},{40,48},{48,56},{56,64},{64,7... | collective-permute-start | bytes 2162696 | tf_op jit(solution)/shard_map/while/body/eval_jaxpr/ppermute | solution.py:12
  291.7 13.1 %collective-permute-start.1 = (bf16[352,1024]{1,0:T(8,128)(2,1)}, bf16[352,1024]{1,0:T(8,128)(2,1)}, u32[]{:S(2)}, u32[]{:S(2)}) collective-permute-start(bf16[352,1024]{1,0:T(8,128)(2,1)} %fusion.49), channel_id=1, source_target_pairs={{0,8},{8,16},{16,24},{24,32},{32,40},{40,48},{48,56},{56,64},{64,7... | collective-permute-start | bytes 2162696 | tf_op jit(solution)/shard_map/while/body/eval_jaxpr/ppermute | solution.py:12
  291.8 20.9 %collective-permute-start = (bf16[352,1024]{1,0:T(8,128)(2,1)S(1)}, bf16[352,1024]{1,0:T(8,128)(2,1)}, u32[]{:S(2)}, u32[]{:S(2)}) collective-permute-start(bf16[352,1024]{1,0:T(8,128)(2,1)S(1)} %copy.18), channel_id=1, source_target_pairs={{0,8},{8,16},{16,24},{24,32},{32,40},{40,48},{48,56},{56,64},{64,7... | collective-permute-start | bytes 2162696 | tf_op jit(solution)/shard_map/while/body/eval_jaxpr/ppermute | solution.py:12
  316.9 13.1 %collective-permute-start.1 = (bf16[352,1024]{1,0:T(8,128)(2,1)}, bf16[352,1024]{1,0:T(8,128)(2,1)}, u32[]{:S(2)}, u32[]{:S(2)}) collective-permute-start(bf16[352,1024]{1,0:T(8,128)(2,1)} %fusion.49), channel_id=1, source_target_pairs={{0,8},{8,16},{16,24},{24,32},{32,40},{40,48},{48,56},{56,64},{64,7... | collective-permute-start | bytes 2162696 | tf_op jit(solution)/shard_map/while/body/eval_jaxpr/ppermute | solution.py:12
  316.9 20.9 %collective-permute-start = (bf16[352,1024]{1,0:T(8,128)(2,1)S(1)}, bf16[352,1024]{1,0:T(8,128)(2,1)}, u32[]{:S(2)}, u32[]{:S(2)}) collective-permute-start(bf16[352,1024]{1,0:T(8,128)(2,1)S(1)} %copy.18), channel_id=1, source_target_pairs={{0,8},{8,16},{16,24},{24,32},{32,40},{40,48},{48,56},{56,64},{64,7... | collective-permute-start | bytes 2162696 | tf_op jit(solution)/shard_map/while/body/eval_jaxpr/ppermute | solution.py:12
  342.1 13.1 %collective-permute-start.1 = (bf16[352,1024]{1,0:T(8,128)(2,1)}, bf16[352,1024]{1,0:T(8,128)(2,1)}, u32[]{:S(2)}, u32[]{:S(2)}) collective-permute-start(bf16[352,1024]{1,0:T(8,128)(2,1)} %fusion.49), channel_id=1, source_target_pairs={{0,8},{8,16},{16,24},{24,32},{32,40},{40,48},{48,56},{56,64},{64,7... | collective-permute-start | bytes 2162696 | tf_op jit(solution)/shard_map/while/body/eval_jaxpr/ppermute | solution.py:12
  342.1 20.9 %collective-permute-start = (bf16[352,1024]{1,0:T(8,128)(2,1)S(1)}, bf16[352,1024]{1,0:T(8,128)(2,1)}, u32[]{:S(2)}, u32[]{:S(2)}) collective-permute-start(bf16[352,1024]{1,0:T(8,128)(2,1)S(1)} %copy.18), channel_id=1, source_target_pairs={{0,8},{8,16},{16,24},{24,32},{32,40},{40,48},{48,56},{56,64},{64,7... | collective-permute-start | bytes 2162696 | tf_op jit(solution)/shard_map/while/body/eval_jaxpr/ppermute | solution.py:12
  367.2 13.1 %collective-permute-start.1 = (bf16[352,1024]{1,0:T(8,128)(2,1)}, bf16[352,1024]{1,0:T(8,128)(2,1)}, u32[]{:S(2)}, u32[]{:S(2)}) collective-permute-start(bf16[352,1024]{1,0:T(8,128)(2,1)} %fusion.49), channel_id=1, source_target_pairs={{0,8},{8,16},{16,24},{24,32},{32,40},{40,48},{48,56},{56,64},{64,7... | collective-permute-start | bytes 2162696 | tf_op jit(solution)/shard_map/while/body/eval_jaxpr/ppermute | solution.py:12
  367.2 20.9 %collective-permute-start = (bf16[352,1024]{1,0:T(8,128)(2,1)S(1)}, bf16[352,1024]{1,0:T(8,128)(2,1)}, u32[]{:S(2)}, u32[]{:S(2)}) collective-permute-start(bf16[352,1024]{1,0:T(8,128)(2,1)S(1)} %copy.18), channel_id=1, source_target_pairs={{0,8},{8,16},{16,24},{24,32},{32,40},{40,48},{48,56},{56,64},{64,7... | collective-permute-start | bytes 2162696 | tf_op jit(solution)/shard_map/while/body/eval_jaxpr/ppermute | solution.py:12
  392.4 13.1 %collective-permute-start.1 = (bf16[352,1024]{1,0:T(8,128)(2,1)}, bf16[352,1024]{1,0:T(8,128)(2,1)}, u32[]{:S(2)}, u32[]{:S(2)}) collective-permute-start(bf16[352,1024]{1,0:T(8,128)(2,1)} %fusion.49), channel_id=1, source_target_pairs={{0,8},{8,16},{16,24},{24,32},{32,40},{40,48},{48,56},{56,64},{64,7... | collective-permute-start | bytes 2162696 | tf_op jit(solution)/shard_map/while/body/eval_jaxpr/ppermute | solution.py:12
  392.4 20.9 %collective-permute-start = (bf16[352,1024]{1,0:T(8,128)(2,1)S(1)}, bf16[352,1024]{1,0:T(8,128)(2,1)}, u32[]{:S(2)}, u32[]{:S(2)}) collective-permute-start(bf16[352,1024]{1,0:T(8,128)(2,1)S(1)} %copy.18), channel_id=1, source_target_pairs={{0,8},{8,16},{16,24},{24,32},{32,40},{40,48},{48,56},{56,64},{64,7... | collective-permute-start | bytes 2162696 | tf_op jit(solution)/shard_map/while/body/eval_jaxpr/ppermute | solution.py:12
  417.6 13.1 %collective-permute-start.1 = (bf16[352,1024]{1,0:T(8,128)(2,1)}, bf16[352,1024]{1,0:T(8,128)(2,1)}, u32[]{:S(2)}, u32[]{:S(2)}) collective-permute-start(bf16[352,1024]{1,0:T(8,128)(2,1)} %fusion.49), channel_id=1, source_target_pairs={{0,8},{8,16},{16,24},{24,32},{32,40},{40,48},{48,56},{56,64},{64,7... | collective-permute-start | bytes 2162696 | tf_op jit(solution)/shard_map/while/body/eval_jaxpr/ppermute | solution.py:12
  417.6 20.9 %collective-permute-start = (bf16[352,1024]{1,0:T(8,128)(2,1)S(1)}, bf16[352,1024]{1,0:T(8,128)(2,1)}, u32[]{:S(2)}, u32[]{:S(2)}) collective-permute-start(bf16[352,1024]{1,0:T(8,128)(2,1)S(1)} %copy.18), channel_id=1, source_target_pairs={{0,8},{8,16},{16,24},{24,32},{32,40},{40,48},{48,56},{56,64},{64,7... | collective-permute-start | bytes 2162696 | tf_op jit(solution)/shard_map/while/body/eval_jaxpr/ppermute | solution.py:12
  442.7 13.1 %collective-permute-start.1 = (bf16[352,1024]{1,0:T(8,128)(2,1)}, bf16[352,1024]{1,0:T(8,128)(2,1)}, u32[]{:S(2)}, u32[]{:S(2)}) collective-permute-start(bf16[352,1024]{1,0:T(8,128)(2,1)} %fusion.49), channel_id=1, source_target_pairs={{0,8},{8,16},{16,24},{24,32},{32,40},{40,48},{48,56},{56,64},{64,7... | collective-permute-start | bytes 2162696 | tf_op jit(solution)/shard_map/while/body/eval_jaxpr/ppermute | solution.py:12
  442.7 20.9 %collective-permute-start = (bf16[352,1024]{1,0:T(8,128)(2,1)S(1)}, bf16[352,1024]{1,0:T(8,128)(2,1)}, u32[]{:S(2)}, u32[]{:S(2)}) collective-permute-start(bf16[352,1024]{1,0:T(8,128)(2,1)S(1)} %copy.18), channel_id=1, source_target_pairs={{0,8},{8,16},{16,24},{24,32},{32,40},{40,48},{48,56},{56,64},{64,7... | collective-permute-start | bytes 2162696 | tf_op jit(solution)/shard_map/while/body/eval_jaxpr/ppermute | solution.py:12
  467.9 13.1 %collective-permute-start.1 = (bf16[352,1024]{1,0:T(8,128)(2,1)}, bf16[352,1024]{1,0:T(8,128)(2,1)}, u32[]{:S(2)}, u32[]{:S(2)}) collective-permute-start(bf16[352,1024]{1,0:T(8,128)(2,1)} %fusion.49), channel_id=1, source_target_pairs={{0,8},{8,16},{16,24},{24,32},{32,40},{40,48},{48,56},{56,64},{64,7... | collective-permute-start | bytes 2162696 | tf_op jit(solution)/shard_map/while/body/eval_jaxpr/ppermute | solution.py:12
  467.9 20.9 %collective-permute-start = (bf16[352,1024]{1,0:T(8,128)(2,1)S(1)}, bf16[352,1024]{1,0:T(8,128)(2,1)}, u32[]{:S(2)}, u32[]{:S(2)}) collective-permute-start(bf16[352,1024]{1,0:T(8,128)(2,1)S(1)} %copy.18), channel_id=1, source_target_pairs={{0,8},{8,16},{16,24},{24,32},{32,40},{40,48},{48,56},{56,64},{64,7... | collective-permute-start | bytes 2162696 | tf_op jit(solution)/shard_map/while/body/eval_jaxpr/ppermute | solution.py:12
  488.7 1.8 copy-start.3
  496.0 1.2 copy-start.1
  496.0 1.6 copy-start.6
  497.6 1.6 copy-start.4
Sparse Core Ops, SparseCore 0:
  10.2 72.6 all-gather.1
  497.3 66.8 reduce-scatter.3
